TPU v7x, 32 devices: a whole 2x2x4 slice. The times are simulated.
32 devices in a mesh: group: 4 (over z), seq: 4 (over y, core), dp: 2 (over x).
Axes of the slice: x: 2, y: 2, z: 4, core: 2. Of those that a mesh axis runs over, the one named last changes fastest.
Arguments:
- noise_gen: bfloat16 [4, 1024, 64], P('dp', 'seq'), may hold values from -6 to 6
- noise_score: bfloat16 [4, 1024, 64], P('dp', 'seq'), may hold values from -6 to 6
- prev_latents: float32 [4, 1024, 64], P('dp', 'seq'), may hold values from -42 to 42
- t_idx: int32 [4], P('dp'), may hold values from 0 to 999
- w_in: bfloat16 [4, 64, 3072], P('group'), may hold values from -4 to 4, as said below
- w_qkv: bfloat16 [4, 3072, 3, 512], P('group', None, None, 'seq'), may hold values from -4 to 4, as said below
- w_out: bfloat16 [4, 512, 64], P('group', 'seq'), may hold values from -4 to 4, as said below
- w_final: bfloat16 [4, 3072, 64], P('group'), may hold values from -4 to 4, as said below
- mod_scale: float32 [4, 3072], P('group'), may hold values from -0.5 to 0.5
- mod_shift: float32 [4, 3072], P('group'), may hold values from -3 to 3
- saved_features: bfloat16 [4, 1024, 3072], P('dp', 'seq'), may hold values from -6 to 6
Outputs:
- predictions: float32 [4, 4, 1024, 64], P('group', 'dp', 'seq')
- dmd_grad: float32 [4, 1024, 64], P('dp', 'seq')
- gen_final_grad: float32 [3072, 64], replicated
Inputs may be any that keep to these rules, and one draw needn't show every extreme that they name: `w_in`: groups 1 and 2 hold equal weights. `w_qkv`: groups 1 and 2 hold equal weights. `w_out`: groups 1 and 2 hold equal weights. `w_final`: groups 1 and 2 hold equal weights.
All inputs are finite; a program needn't handle non-finite values. Where the computation divides by a largest or mean magnitude, that divisor is 1e-20 or more.
Results may differ from a plain program's by a relative error of at most 0.017.
Values may be sent and summed in bfloat16 or wider, within the bound.
A program may use at most 128 MiB of HBM per device.

v0:
```python
import math

import jax
import jax.numpy as jnp
from jax import lax
from jax.sharding import PartitionSpec as P

NTOK = 1024
NOISE_LEVEL_COUNT = 1000


def embed(latent, noise_level, w_in_here, scale, shift):
    projected = jnp.einsum("inp,pd->ind", latent, w_in_here, preferred_element_type=jnp.float32)
    normed = projected * lax.rsqrt(jnp.mean(projected * projected, axis=-1, keepdims=True) + 1e-06)
    return (normed * (1.0 + noise_level[:, None, None] * scale) + shift).astype(jnp.bfloat16)


def per_device(
    noise_gen,
    noise_score,
    prev_latents,
    t_idx,
    w_in,
    w_qkv,
    w_out,
    w_final,
    mod_scale,
    mod_shift,
    saved_features,
):
    model_index = lax.axis_index("group")
    local_image_batch, rows_image, channels = noise_gen.shape
    width = w_in.shape[2]
    head_size = w_out.shape[1]
    level = (t_idx.astype(jnp.float32) + 0.5) / NOISE_LEVEL_COUNT
    noisy = (1.0 - level)[:, None, None] * prev_latents + level[:, None, None] * noise_score.astype(
        jnp.float32
    )
    is_generator = model_index == 0
    model_input = jnp.where(is_generator, noise_gen.astype(jnp.float32), noisy)
    noise_level = jnp.where(is_generator, jnp.ones_like(level), level)
    latent = model_input.astype(jnp.bfloat16)
    w_in_here = w_in[0]
    head_weight = w_qkv[0].reshape(width, 3 * head_size)
    scale = mod_scale[0]
    shift = mod_shift[0]
    features = embed(latent, noise_level, w_in_here, scale, shift)
    triple = jnp.einsum(
        "ind,de->ine",
        lax.all_gather(features, "seq", axis=1, tiled=True),
        head_weight,
        preferred_element_type=jnp.float32,
    ).astype(jnp.bfloat16)
    queries = triple[:, :, :head_size]
    keys = triple[:, :, head_size : 2 * head_size]
    value_rows = triple[:, :, 2 * head_size :]
    scores = jnp.einsum(
        "iqe,ike->iqk", queries, keys, preferred_element_type=jnp.float32
    ) / math.sqrt(head_size)
    probs = jax.nn.softmax(scores, axis=-1).astype(jnp.bfloat16)
    attention_result = jnp.einsum(
        "iqk,ike->iqe", probs, value_rows, preferred_element_type=jnp.float32
    ).astype(jnp.bfloat16)
    token_leading_layout = attention_result.transpose(1, 0, 2)
    output_layout = w_out[0]
    summed = (
        lax.psum_scatter(
            jnp.einsum(
                "sca,af->scf",
                token_leading_layout,
                output_layout,
                preferred_element_type=jnp.float32,
            ).astype(jnp.bfloat16),
            "seq",
            scatter_dimension=0,
            tiled=True,
        )
        .astype(jnp.float32)
        .transpose(1, 0, 2)
    )
    velocity = (
        jnp.einsum("ind,dp->inp", features, w_final[0], preferred_element_type=jnp.float32) + summed
    )
    prediction = model_input - noise_level[:, None, None] * velocity
    real_weight = jnp.where(model_index == 1, 2.5, jnp.where(model_index == 2, -1.5, 0.0))
    fake_weight = jnp.where(model_index == 3, 1.0, 0.0)
    real, fake = lax.psum((real_weight * prediction, fake_weight * prediction), "group")
    deviation = jnp.sum(jnp.abs(prev_latents - real), axis=(1, 2))
    total_dev = lax.psum(deviation, "seq")
    spread = total_dev / (NTOK * channels) + 1e-05
    dmd_grad = (fake - real) / spread[:, None, None]
    down = (-dmd_grad).astype(jnp.bfloat16)
    normalizer = 1.0 / math.sqrt(local_image_batch * lax.axis_size("dp") * NTOK)
    partial_grad = jnp.einsum(
        "ind,inp->dp", saved_features, down, preferred_element_type=jnp.float32
    )
    total_grad = lax.psum(partial_grad, ("seq", "dp"))
    return (prediction[None], dmd_grad, total_grad * normalizer)


def solution(mesh):
    placed = (
        P("dp", "seq", None),
        P("dp", "seq", None),
        P("dp", "seq", None),
        P("dp"),
        P("group", None, None),
        P("group", None, None, "seq"),
        P("group", "seq", None),
        P("group", None, None),
        P("group", None),
        P("group", None),
        P("dp", "seq", None),
    )
    return jax.shard_map(
        per_device,
        mesh=mesh,
        in_specs=placed,
        out_specs=(P("group", "dp", "seq", None), P("dp", "seq", None), P()),
        check_vma=False,
    )
```

profile of v0, /device:TPU:1, one launch (start us, length us, event | category | flops | bytes accessed | tf_op | source)
XLA Modules:
  0.0 254.6 jit_solution(11560550271201189968)
XLA Ops:
  7.2 0.0 copy-start
  7.2 0.0 copy-start.6
  7.2 0.0 copy-start.5
  7.2 0.0 all-gather.2.cloned.1.call-start
  7.3 0.8 broadcast_select_fusion
  8.1 2.4 multiply_reduce_fusion.1
  10.5 0.0 copy-done.6
  10.5 0.1 multiply_add_fusion
  10.5 0.0 copy-done.5
  10.5 2.8 %add_convert_fusion = bf16[2,256,3072]{2,1,0:T(8,128)(2,1)} fusion(f32[2,256,3072]{2,1,0:T(8,128)S(1)} %get-tuple-element.11, f32[3072]{0:T(1024)S(1)} %bitcast.40, f32[2,3072]{1,0:T(2,128)S(1)} %multiply_add_fusion, f32[2,256]{1,0:T(2,128)S(1)} %add_rsqrt_fusion), kind=kLoop, calls=%fused_computation.5 | loop fusion | flops 6291456 | bytes 9476096 | tf_op jit(solution)/shard_map/convert_element_type | solution.py:15
  13.4 0.0 all-gather.2.cloned.1.call-update
  13.4 0.0 reduce-scatter.2.cloned.1.call-start
  13.4 4.3 %copy.14 = bf16[1,3072,3,128]{1,3,2,0:T(8,128)(2,1)} copy(bf16[1,3072,3,128]{3,1,2,0:T(8,128)(2,1)} %param.16) | data formatting | bytes 4718592 | tf_op args[5]
  17.7 80.4 %all-gather.2.cloned.1.call-done = bf16[2,1024,3072]{2,1,0:T(8,128)(2,1)} async-done(((bf16[2,256,3072]{2,1,0:T(8,128)(2,1)}), bf16[2,1024,3072]{2,1,0:T(8,128)(2,1)}) %all-gather.2.cloned.1.call-update) | async-done | bytes 12582928 | tf_op jit(solution)/shard_map/all_gather | solution.py:50
  98.2 11.2 %convolution_convert_fusion = bf16[2,1024,384]{2,1,0:T(8,128)(2,1)} fusion(bf16[2,1024,3072]{2,1,0:T(8,128)(2,1)} %all-gather.2.cloned.1.call-done, bf16[3072,384,1]{0,1,2:T(8,128)(2,1)} %bitcast.38), kind=kOutput, calls=%fused_computation.10 | convolution fusion | flops 4832624640 | bytes 16515072 | tf_op jit(solution)/shard_map/ind,de->ine/dot_general | solution.py:48
  109.4 0.0 copy-start.7
  109.4 7.1 %fusion.33 = (f32[2,1024]{1,0:T(2,128)S(1)}, f32[2,1024,1024]{1,2,0:T(8,128)}) fusion(bf16[2,1024,384]{2,1,0:T(8,128)(2,1)} %convolution_convert_fusion), kind=kOutput, calls=%fused_computation.44 | convolution fusion | flops 543163392 | bytes 9445376 | tf_op jit(solution)/shard_map/sub | solution.py:60
  116.5 0.0 copy-done.7
  116.5 0.0 copy-start.1
  116.5 0.0 copy-start.2
  116.6 0.0 copy-start.3
  116.6 6.0 %fusion.9 = bf16[1024,2,64]{0,2,1:T(8,128)(2,1)} fusion(f32[2,1024,1024]{1,2,0:T(8,128)} %get-tuple-element.13, f32[2,1024]{1,0:T(2,128)S(1)} %get-tuple-element.12, bf16[2,1024,384]{2,1,0:T(8,128)(2,1)} %convolution_convert_fusion, bf16[1,128,64]{1,2,0:T(8,128)(2,1)S(1)} %copy-done.7), kind=kOutput, calls=%fused_computation.14 | convolution fusion | flops 575012864 | bytes 9199616 | tf_op jit(solution)/shard_map/sca,af->scf/dot_general | solution.py:68
  122.6 0.0 reduce-scatter.2.cloned.1.call-update
  122.6 0.0 all-reduce.6.cloned.1.call-start
  122.7 19.7 %reduce-scatter.2.cloned.1.call-done = bf16[256,2,64]{0,2,1:T(8,128)(2,1)} async-done(((bf16[1024,2,64]{0,2,1:T(8,128)(2,1)}), bf16[256,2,64]{0,2,1:T(8,128)(2,1)}) %reduce-scatter.2.cloned.1.call-update) | async-done | bytes 65552 | tf_op jit(solution)/shard_map/reduce_scatter | solution.py:67
  142.3 0.0 copy-done.1
  142.3 0.0 copy-done.2
  142.3 0.0 copy-done.3
  142.3 3.9 %broadcast_multiply_fusion.1 = (f32[2,256,64]{1,2,0:T(8,128)}, f32[2,256,64]{1,2,0:T(8,128)}, f32[2,256,64]{1,2,0:T(8,128)}) fusion(f32[]{:T(128)S(6)} %select_n.33, f32[]{:T(128)S(6)} %select_n.31, bf16[256,2,64]{0,2,1:T(8,128)(2,1)} %reduce-scatter.2.cloned.1.call-done, bf16[2,256,3072]{2,1,0:T(8,128)(2,1)} %add_convert_fusion, ...), kind=kOutput, calls=%fused_computation.33 | convolution fusion | flops 201719808 | bytes 4259873 | tf_op jit(solution)/shard_map/ind,dp->inp/dot_general | solution.py:82
  146.2 0.0 all-reduce.6.cloned.1.call-update
  146.2 0.0 all-reduce.4.cloned.1.call-start
  146.3 34.2 %all-reduce.6.cloned.1.call-done = (f32[2,256,64]{1,2,0:T(8,128)}, f32[2,256,64]{1,2,0:T(8,128)}) async-done(((f32[2,256,64]{1,2,0:T(8,128)}, f32[2,256,64]{1,2,0:T(8,128)}), (f32[2,256,64]{1,2,0:T(8,128)}, f32[2,256,64]{1,2,0:T(8,128)})) %all-reduce.6.cloned.1.call-update) | async-done | bytes 262160 | tf_op jit(solution)/shard_map/psum | solution.py:87
  180.5 1.0 abs_reduce_fusion
  181.5 7.1 %psum.30 = f32[2]{0:T(128)S(1)} all-reduce(f32[2]{0:T(128)S(1)} %abs_reduce_fusion), channel_id=1, replica_groups=mesh['group'=4,'seq'=4,'dp'=2] {'seq'}, use_global_device_ids=true, to_apply=%region_7.8 | all-reduce | flops 2 | bytes 16 | tf_op jit(solution)/shard_map/psum | solution.py:89
  188.6 1.0 subtract_divide_fusion
  189.7 0.0 copy-done
  189.7 0.0 copy-start.4
  189.7 1.5 convolution_bitcast_fusion
  191.2 0.0 all-reduce.4.cloned.1.call-update
  191.3 54.7 %all-reduce.4.cloned.1.call-done = f32[3072,64]{0,1:T(8,128)} async-done(((f32[3072,64]{0,1:T(8,128)}), f32[3072,64]{0,1:T(8,128)}) %all-reduce.4.cloned.1.call-update) | async-done | bytes 786448 | tf_op jit(solution)/shard_map/psum | solution.py:97
  246.0 2.1 broadcast_multiply_fusion
  248.0 0.0 copy-done.4
  (2 shorter events, 0.0 us)
Async XLA Ops:
  7.2 182.5 %copy-start = (bf16[2,256,3072]{2,1,0:T(8,128)(2,1)S(1)}, bf16[2,256,3072]{2,1,0:T(8,128)(2,1)}, u32[]{:S(2)}) copy-start(bf16[2,256,3072]{2,1,0:T(8,128)(2,1)} %param.21) | copy-start | bytes 9437188
  7.2 3.3 %copy-start.6 = (f32[1,3072]{1,0:T(1,128)S(1)}, f32[1,3072]{1,0:T(1,128)}, u32[]{:S(2)}) copy-start(f32[1,3072]{1,0:T(1,128)} %param.19) | copy-start | bytes 36868
  7.2 3.4 %copy-start.5 = (f32[1,3072]{1,0:T(1,128)S(1)}, f32[1,3072]{1,0:T(1,128)}, u32[]{:S(2)}) copy-start(f32[1,3072]{1,0:T(1,128)} %param.20) | copy-start | bytes 36868
  7.2 91.0 %all-gather.2.cloned.1.call-start = ((), (), s32[]{:S(2)}) async-start(), calls=%async_computation.1 | async-start | bytes 15728640 | tf_op jit(solution)/shard_map/all_gather | solution.py:50
  13.4 128.9 %reduce-scatter.2.cloned.1.call-start = ((), (), s32[]{:S(2)}) async-start(), calls=%async_computation.2 | async-start | bytes 327680 | tf_op jit(solution)/shard_map/reduce_scatter | solution.py:67
  109.4 7.1 %copy-start.7 = (bf16[1,128,64]{1,2,0:T(8,128)(2,1)S(1)}, bf16[1,128,64]{1,2,0:T(8,128)(2,1)}, u32[]{:S(2)}) copy-start(bf16[1,128,64]{1,2,0:T(8,128)(2,1)} %param.17) | copy-start | bytes 49156
  116.5 25.8 %copy-start.1 = (f32[2,256,64]{1,2,0:T(8,128)S(1)}, f32[2,256,64]{1,2,0:T(8,128)}, u32[]{:S(2)}) copy-start(f32[2,256,64]{1,2,0:T(8,128)} %param.13) | copy-start | bytes 393220
  116.5 25.8 %copy-start.2 = (bf16[2,256,64]{1,2,0:T(8,128)(2,1)S(1)}, bf16[2,256,64]{1,2,0:T(8,128)(2,1)}, u32[]{:S(2)}) copy-start(bf16[2,256,64]{1,2,0:T(8,128)(2,1)} %param.12) | copy-start | bytes 196612
  116.6 25.8 %copy-start.3 = (bf16[2,256,64]{1,2,0:T(8,128)(2,1)S(1)}, bf16[2,256,64]{1,2,0:T(8,128)(2,1)}, u32[]{:S(2)}) copy-start(bf16[2,256,64]{1,2,0:T(8,128)(2,1)} %param.11) | copy-start | bytes 196612
  122.6 57.9 %all-reduce.6.cloned.1.call-start = ((), (), s32[]{:S(2)}) async-start(), calls=%async_computation.4 | async-start | bytes 524288 | tf_op jit(solution)/shard_map/psum | solution.py:87
  146.2 99.8 %all-reduce.4.cloned.1.call-start = ((), (), s32[]{:S(2)}) async-start(), calls=%async_computation.3 | async-start | bytes 1572864 | tf_op jit(solution)/shard_map/psum | solution.py:97
  189.7 58.3 %copy-start.4 = (f32[2,256,64]{1,2,0:T(8,128)}, f32[2,256,64]{1,2,0:T(8,128)S(1)}, u32[]{:S(2)}) copy-start(f32[2,256,64]{1,2,0:T(8,128)S(1)} %subtract_divide_fusion) | copy-start | bytes 393220
Sparse Core Ops, SparseCore 0:
  13.5 84.6 all-gather.1
  122.7 19.5 reduce-scatter.1
  146.3 34.0 all-reduce.5
  191.4 54.5 all-reduce.3
where the time goes:
time: 257 us; the launch traced here: 255 us
  waiting for transfers between devices  189 us (74%)
  matrix products  32.2 us (13%)
  between operations  13.9 us (5%)
  other arithmetic  7.86 us (3%)
  blocking collectives  7.14 us (3%)
  local copies, waits for them, and re-layouts  4.35 us (2%)
    all_gather x1, waiting for transfers between devices, per_device(): lax.all_gather(features, 'seq', axis=1, tiled=True)  80.4 us
    psum x1, waiting for transfers between devices, per_device(): total_grad = lax.psum(partial_grad, ('seq', 'dp'))  54.7 us
    psum x1, waiting for transfers between devices, per_device(): lax.psum((real_weight * prediction, fake_weight * prediction), 'group')  34.2 us
    reduce_scatter x1, waiting for transfers between devices, per_device(): lax.psum_scatter(jnp.einsum('sca,af->scf', token_leading_layout, output_l...  19.7 us
    dot_general x1, matrix products, per_device(): jnp.einsum('ind,de->ine', lax.all_gather(features, 'seq', axis=1, tiled=T...  11.2 us
    sub x1, matrix products, per_device(): probs = jax.nn.softmax(scores, axis=-1).astype(jnp.bfloat16)  7.14 us
    psum x1, blocking collectives, per_device(): total_dev = lax.psum(deviation, 'seq')  7.14 us
    dot_general x1, matrix products, per_device(): jnp.einsum('sca,af->scf', token_leading_layout, output_layout, preferred_...  6 us
  transfers between devices with their start and end apart: 4, of which 4 were waited for; matrix products, arithmetic and copies ran while one was open for 2% of the time, Pallas kernels for 0%

commit v1 on v0

--- a/solution.py
+++ b/solution.py
@@ -1,8 +1,11 @@
+import functools
 import math
 
 import jax
 import jax.numpy as jnp
 from jax import lax
+from jax.experimental import pallas as pl
+from jax.experimental.pallas import tpu as pltpu
 from jax.sharding import PartitionSpec as P
 
 NTOK = 1024
@@ -15,7 +18,7 @@
     return (normed * (1.0 + noise_level[:, None, None] * scale) + shift).astype(jnp.bfloat16)
 
 
-def per_device(
+def per_device_plain(
     noise_gen,
     noise_score,
     prev_latents,
@@ -98,6 +101,497 @@
     return (prediction[None], dmd_grad, total_grad * normalizer)
 
 
+F32 = jnp.float32
+BF16 = jnp.bfloat16
+MESH = pl.DeviceIdType.MESH
+PARTS = 3
+ROWS = 16
+
+
+def dot(a, b):
+    return jnp.dot(a, b, preferred_element_type=F32)
+
+
+def dot_first(a, b):
+    return lax.dot_general(a, b, (((0,), (0,)), ((), ())), preferred_element_type=F32)
+
+
+def dot_last(a, b):
+    return lax.dot_general(a, b, (((1,), (1,)), ((), ())), preferred_element_type=F32)
+
+
+def split_parts(x):
+    terms = []
+    for _ in range(PARTS):
+        term = x.astype(BF16)
+        terms.append(term)
+        x = x - term.astype(F32)
+    return terms
+
+
+def kernel(
+    dims,
+    t_ref,
+    noise_gen_ref,
+    noise_score_ref,
+    prev_ref,
+    w_in_ref,
+    w_qkv_hbm,
+    w_out_ref,
+    w_final_hbm,
+    scale_ref,
+    shift_ref,
+    saved_hbm,
+    pred_ref,
+    dmd_ref,
+    grad_ref,
+    w_qkv,
+    w_final,
+    saved,
+    left,
+    xg,
+    rg,
+    noisy,
+    keys,
+    queries,
+    values,
+    vel_out,
+    vel_in,
+    split_out,
+    split_in,
+    diff,
+    dev,
+    grad_out,
+    grad_in,
+    gathered,
+    load_sem,
+    x_send,
+    x_recv,
+    r_send,
+    r_recv,
+    vel_send,
+    vel_recv,
+    split_send,
+    split_recv,
+    diff_send,
+    diff_recv,
+    dev_send,
+    dev_recv,
+    grad_send,
+    grad_recv,
+    up_send,
+    up_recv,
+    all_send,
+    all_recv,
+):
+    n_group, n_seq, n_dp = dims
+    n_plane = n_seq * n_dp
+    images, channels, toks = prev_ref.shape
+    width = w_in_ref.shape[1]
+    head = w_out_ref.shape[1]
+    share = saved.shape[2]
+    chunk = grad_in.shape[2]
+    lane_blocks = share // chunk
+    g = lax.axis_index("group")
+    s = lax.axis_index("seq")
+    d = lax.axis_index("dp")
+    here = g * n_seq + s
+    place = s * n_dp + d
+
+    loads = [
+        pltpu.make_async_copy(w_qkv_hbm, w_qkv, load_sem.at[0]),
+        pltpu.make_async_copy(w_final_hbm, w_final, load_sem.at[1]),
+        pltpu.make_async_copy(
+            saved_hbm.at[:, :, pl.ds(pl.multiple_of(g * share, 128), share)], saved, load_sem.at[2]
+        ),
+    ]
+    for load in loads:
+        load.start()
+
+    barrier = pltpu.get_barrier_semaphore()
+    peers = 0
+    for dg in range(n_group):
+        for ds in range(n_seq):
+            if dg or ds:
+                pl.semaphore_signal(
+                    barrier,
+                    inc=1,
+                    device_id={"group": lax.rem(g + dg, n_group), "seq": lax.rem(s + ds, n_seq)},
+                    device_id_type=MESH,
+                )
+                peers += 1
+    for ds in range(n_seq):
+        for dd in range(1, n_dp):
+            pl.semaphore_signal(
+                barrier,
+                inc=1,
+                device_id={"seq": lax.rem(s + ds, n_seq), "dp": lax.rem(d + dd, n_dp)},
+                device_id_type=MESH,
+            )
+            peers += 1
+
+    generator = jnp.where(g == 0, 1.0, 0.0).astype(F32)
+
+    def level(i, lanes):
+        return (jnp.full((1, lanes), t_ref[i].astype(F32), F32) + 0.5) / NOISE_LEVEL_COUNT
+
+    def own_level(i, lanes):
+        return generator + (1.0 - generator) * level(i, lanes)
+
+    for i in range(images):
+        lv = level(i, toks)
+        noisy[i] = (1.0 - lv) * prev_ref[i] + lv * noise_score_ref[i].astype(F32)
+        model_input = generator * noise_gen_ref[i].astype(F32) + (1.0 - generator) * noisy[i]
+        pred_ref[i] = model_input
+        xg[0, i] = model_input.astype(BF16)
+
+    pl.semaphore_wait(barrier, peers)
+
+    sends = []
+
+    def send(src, dst, send_sem, recv_sem, device):
+        copy = pltpu.make_async_remote_copy(
+            src_ref=src,
+            dst_ref=dst,
+            send_sem=send_sem,
+            recv_sem=recv_sem,
+            device_id=device,
+            device_id_type=MESH,
+        )
+        copy.start()
+        sends.append(copy)
+
+    def arrive(dst, send_sem, recv_sem, device):
+        pltpu.make_async_remote_copy(
+            src_ref=dst,
+            dst_ref=dst,
+            send_sem=send_sem,
+            recv_sem=recv_sem,
+            device_id=device,
+            device_id_type=MESH,
+        ).wait_recv()
+
+    def seq_peer(k):
+        return {"seq": lax.rem(s + k, n_seq)}
+
+    for k in range(1, n_seq):
+        send(xg.at[0], xg.at[k], x_send.at[k], x_recv.at[k], seq_peer(n_seq - k))
+
+    both = jnp.concatenate([xg[0, i] for i in range(images)], axis=1)
+    square = jnp.zeros((1, images * toks), F32)
+    step = width // 4
+    for at in range(0, width, step):
+        projected = dot_first(w_in_ref[:, at : at + step], both)
+        square = square + jnp.sum(projected * projected, axis=0, keepdims=True)
+    inverse = lax.rsqrt(square * (1.0 / width) + 1e-06)
+    rg[0] = jnp.concatenate(
+        [inverse[:, i * toks : (i + 1) * toks] for i in range(images)]
+        + [jnp.zeros((8 - images, toks), F32)],
+        axis=0,
+    )
+    for k in range(1, n_seq):
+        send(rg.at[0], rg.at[k], r_send.at[k], r_recv.at[k], seq_peer(n_seq - k))
+
+    left[0:channels] = w_in_ref[...]
+    scaled = split_parts(w_in_ref[...].astype(F32) * scale_ref[...])
+    for at, term in enumerate(scaled):
+        left[(at + 1) * channels : (at + 2) * channels] = term
+    base = (PARTS + 1) * channels
+    row = lax.broadcasted_iota(jnp.int32, (ROWS, width), 0)
+    shift_rows = jnp.zeros((ROWS, width), F32)
+    for at, term in enumerate(split_parts(shift_ref[...])):
+        shift_rows = jnp.where(row == at, term.astype(F32), shift_rows)
+    left[base : base + ROWS] = shift_rows.astype(BF16)
+
+    loads[0].wait()
+    loads[1].wait()
+    maps = [dot(left[...], w_qkv[c]) for c in range(3)] + [dot_last(left[...], w_final[...])]
+    maps = jnp.concatenate(maps, axis=1)
+    total = 3 * head + channels
+    plain = maps[0:channels]
+    per_level = sum(maps[(at + 1) * channels : (at + 2) * channels] for at in range(PARTS))
+    bias_row = jnp.sum(maps[base : base + ROWS], axis=0, keepdims=True)
+    row = lax.broadcasted_iota(jnp.int32, (ROWS, total), 0)
+    bias_rows = jnp.zeros((ROWS, total), F32)
+    for at, term in enumerate(split_parts(bias_row)):
+        bias_rows = jnp.where(row == at, term.astype(F32), bias_rows)
+    bias = dot_first(bias_rows.astype(BF16), jnp.ones((ROWS, toks), BF16))
+    combined = [
+        jnp.concatenate(split_parts(plain + own_level(i, total) * per_level), axis=0)
+        for i in range(images)
+    ]
+
+    factor = math.log2(math.e) / math.sqrt(head)
+    local = []
+    for k in range(n_seq):
+        if k:
+            arrive(xg.at[k], x_send.at[k], x_recv.at[k], seq_peer(k))
+            arrive(rg.at[k], r_send.at[k], r_recv.at[k], seq_peer(k))
+        rows = total if k == 0 else 3 * head
+        for i in range(images):
+            x = xg[k, i]
+            stacked = jnp.concatenate([x] * PARTS, axis=0)
+            triple = dot_first(combined[i][:, :rows], stacked) * rg[k, i : i + 1, :] + bias[:rows]
+            queries[i, k] = (triple[:head] * factor).astype(BF16)
+            keys[i, k * toks : (k + 1) * toks] = triple[head : 2 * head].T.astype(BF16)
+            values[i, :, k * toks : (k + 1) * toks] = triple[2 * head : 3 * head].astype(BF16)
+            if k == 0:
+                local.append(triple[3 * head :])
+
+    own = []
+    for k in list(range(1, n_seq)) + [0]:
+        for i in range(images):
+            scores = dot(keys[i], queries[i, k])
+            weights = jnp.exp2(scores - jnp.max(scores, axis=0, keepdims=True))
+            norm = 1.0 / jnp.sum(weights, axis=0, keepdims=True)
+            attended = (dot(values[i], weights.astype(BF16)) * norm).astype(BF16)
+            term = dot(w_out_ref[...], attended)
+            if k:
+                vel_out[k, i] = term.astype(BF16)
+            else:
+                own.append(term)
+        if k:
+            send(vel_out.at[k], vel_in.at[k], vel_send.at[k], vel_recv.at[k], seq_peer(k))
+
+    for k in range(1, n_seq):
+        arrive(vel_in.at[k], vel_send.at[k], vel_recv.at[k], seq_peer(n_seq - k))
+    for i in range(images):
+        velocity = local[i] + own[i]
+        for k in range(1, n_seq):
+            velocity = velocity + vel_in[k, i].astype(F32)
+        pred_ref[i] = pred_ref[i] - own_level(i, toks) * velocity
+        for h in range(n_group):
+            split_out[h, i] = velocity[h * ROWS : (h + 1) * ROWS].astype(BF16)
+
+    def group_peer(k):
+        return {"group": lax.rem(g + k, n_group)}
+
+    for k in range(1, n_group):
+        to = lax.rem(g + k, n_group)
+        send(split_out.at[to], split_in.at[g], split_send.at[k], split_recv.at[g], group_peer(k))
+    split_in[g] = split_out[g]
+    for k in range(1, n_group):
+        frm = lax.rem(g + k, n_group)
+        arrive(split_in.at[frm], split_send.at[k], split_recv.at[frm], group_peer(k))
+
+    part = pl.ds(pl.multiple_of(g * ROWS, ROWS), ROWS)
+    sums = []
+    for i in range(images):
+        lv = level(i, toks)
+        guided = 2.5 * split_in[1, i].astype(F32) - 1.5 * split_in[2, i].astype(F32)
+        real = noisy[i, part, :] - lv * guided
+        away = jnp.abs(prev_ref[i, part, :] - real)
+        away = jnp.sum(jnp.sum(away, axis=0, keepdims=True), axis=1, keepdims=True)
+        sums.append(jnp.broadcast_to(away, (1, 128)))
+        diff[i, part, :] = (lv * (guided - split_in[3, i].astype(F32))).astype(BF16)
+    dev[here] = jnp.concatenate(sums + [jnp.zeros((8 - images, 128), F32)], axis=0)
+    for k in range(1, n_group):
+        send(diff.at[:, part, :], diff.at[:, part, :], diff_send.at[k], diff_recv.at[g], group_peer(k))
+    for dg in range(n_group):
+        for ds in range(n_seq):
+            if dg or ds:
+                send(
+                    dev.at[here],
+                    dev.at[here],
+                    dev_send.at[dg * n_seq + ds],
+                    dev_recv.at[here],
+                    {"group": lax.rem(g + dg, n_group), "seq": lax.rem(s + ds, n_seq)},
+                )
+    loads[2].wait()
+    for k in range(1, n_group):
+        frm = lax.rem(g + k, n_group)
+        theirs = diff.at[:, pl.ds(pl.multiple_of(frm * ROWS, ROWS), ROWS), :]
+        arrive(theirs, diff_send.at[k], diff_recv.at[frm], group_peer(k))
+    products = [dot(diff[i], saved[i]) for i in range(images)]
+    for dg in range(n_group):
+        for ds in range(n_seq):
+            if dg or ds:
+                there = lax.rem(g + dg, n_group) * n_seq + lax.rem(s + ds, n_seq)
+                arrive(
+                    dev.at[there],
+                    dev_send.at[dg * n_seq + ds],
+                    dev_recv.at[there],
+                    {"group": lax.rem(g + dg, n_group), "seq": lax.rem(s + ds, n_seq)},
+                )
+    away = dev[0]
+    for at in range(1, n_group * n_seq):
+        away = away + dev[at]
+    spread = away * (1.0 / (n_seq * toks * channels)) + 1e-05
+    gradient = 0.0
+    for i in range(images):
+        over = 1.0 / spread[i : i + 1, 0:1]
+        gradient = gradient - products[i] * over
+        dmd_ref[i] = diff[i].astype(F32) * over
+    for o in range(n_plane):
+        r0, c0 = (o // lane_blocks) * ROWS, (o % lane_blocks) * chunk
+        grad_out[o] = gradient[r0 : r0 + ROWS, c0 : c0 + chunk].astype(BF16)
+
+    def plane_peer(k):
+        to = lax.rem(place + k, n_plane)
+        return to, {"seq": to // n_dp, "dp": lax.rem(to, n_dp)}
+
+    for k in range(1, n_plane):
+        to, device = plane_peer(k)
+        send(grad_out.at[to], grad_in.at[k], grad_send.at[k], grad_recv.at[k], device)
+    summed = grad_out[place].astype(F32)
+    for k in range(1, n_plane):
+        arrive(grad_in.at[k], grad_send.at[k], grad_recv.at[k], plane_peer(n_plane - k)[1])
+        summed = summed + grad_in[k].astype(F32)
+    normalizer = 1.0 / math.sqrt(images * n_dp * n_seq * toks)
+    gathered[place, g] = (summed * normalizer).astype(BF16)
+    for k in range(1, n_group):
+        send(gathered.at[place, g], gathered.at[place, g], up_send.at[k], up_recv.at[g], group_peer(k))
+    for k in range(1, n_group):
+        frm = lax.rem(g + k, n_group)
+        arrive(gathered.at[place, frm], up_send.at[k], up_recv.at[frm], group_peer(k))
+    for k in range(1, n_plane):
+        to, device = plane_peer(k)
+        send(gathered.at[place], gathered.at[place], all_send.at[k], all_recv.at[place], device)
+    for k in range(1, n_plane):
+        frm, device = plane_peer(k)
+        arrive(gathered.at[frm], all_send.at[k], all_recv.at[frm], device)
+    for o in range(n_plane):
+        r0 = (o // lane_blocks) * ROWS
+        for h in range(n_group):
+            c0 = h * share + (o % lane_blocks) * chunk
+            grad_ref[r0 : r0 + ROWS, c0 : c0 + chunk] = gathered[o, h].astype(F32)
+    for copy in sends:
+        copy.wait_send()
+
+
+def fits(shape, images, toks, channels, width, head):
+    n_group, n_plane = shape["group"], shape["seq"] * shape["dp"]
+    row_blocks = channels // ROWS
+    return (
+        n_group == 4
+        and channels == n_group * ROWS
+        and images <= 8
+        and toks % 128 == 0
+        and head % 128 == 0
+        and n_plane % row_blocks == 0
+        and width % (n_group * (n_plane // row_blocks) * 128) == 0
+    )
+
+
+def per_device(
+    shape,
+    noise_gen,
+    noise_score,
+    prev_latents,
+    t_idx,
+    w_in,
+    w_qkv,
+    w_out,
+    w_final,
+    mod_scale,
+    mod_shift,
+    saved_features,
+):
+    images, toks, channels = noise_gen.shape
+    width, head = w_in.shape[2], w_out.shape[1]
+    if not fits(shape, images, toks, channels, width, head):
+        return per_device_plain(
+            noise_gen,
+            noise_score,
+            prev_latents,
+            t_idx,
+            w_in,
+            w_qkv,
+            w_out,
+            w_final,
+            mod_scale,
+            mod_shift,
+            saved_features,
+        )
+    n_group, n_seq, n_dp = shape["group"], shape["seq"], shape["dp"]
+    n_plane = n_seq * n_dp
+    share = width // n_group
+    chunk = share // (n_plane // (channels // ROWS))
+    vmem = pl.BlockSpec(memory_space=pltpu.VMEM)
+    anywhere = pl.BlockSpec(memory_space=pl.ANY)
+    dma = pltpu.SemaphoreType.DMA
+    all_tokens = n_seq * toks
+    total_in = n_group * n_seq
+    prediction, dmd_grad, grad = pl.pallas_call(
+        functools.partial(kernel, (n_group, n_seq, n_dp)),
+        out_shape=(
+            jax.ShapeDtypeStruct((images, channels, toks), F32),
+            jax.ShapeDtypeStruct((images, channels, toks), F32),
+            jax.ShapeDtypeStruct((channels, width), F32),
+        ),
+        in_specs=[
+            pl.BlockSpec(memory_space=pltpu.SMEM),
+            vmem,
+            vmem,
+            vmem,
+            vmem,
+            anywhere,
+            vmem,
+            anywhere,
+            vmem,
+            vmem,
+            anywhere,
+        ],
+        out_specs=(vmem, vmem, vmem),
+        scratch_shapes=[
+            pltpu.VMEM((3, width, head), BF16),
+            pltpu.VMEM((channels, width), BF16),
+            pltpu.VMEM((images, toks, share), BF16),
+            pltpu.VMEM(((PARTS + 1) * channels + ROWS, width), BF16),
+            pltpu.VMEM((n_seq, images, channels, toks), BF16),
+            pltpu.VMEM((n_seq, 8, toks), F32),
+            pltpu.VMEM((images, channels, toks), F32),
+            pltpu.VMEM((images, all_tokens, head), BF16),
+            pltpu.VMEM((images, n_seq, head, toks), BF16),
+            pltpu.VMEM((images, head, all_tokens), BF16),
+            pltpu.VMEM((n_seq, images, channels, toks), BF16),
+            pltpu.VMEM((n_seq, images, channels, toks), BF16),
+            pltpu.VMEM((n_group, images, ROWS, toks), BF16),
+            pltpu.VMEM((n_group, images, ROWS, toks), BF16),
+            pltpu.VMEM((images, channels, toks), BF16),
+            pltpu.VMEM((total_in, 8, 128), F32),
+            pltpu.VMEM((n_plane, ROWS, chunk), BF16),
+            pltpu.VMEM((n_plane, ROWS, chunk), BF16),
+            pltpu.VMEM((n_plane, n_group, ROWS, chunk), BF16),
+            dma((3,)),
+            dma((n_seq,)),
+            dma((n_seq,)),
+            dma((n_seq,)),
+            dma((n_seq,)),
+            dma((n_seq,)),
+            dma((n_seq,)),
+            dma((n_group,)),
+            dma((n_group,)),
+            dma((n_group,)),
+            dma((n_group,)),
+            dma((total_in,)),
+            dma((total_in,)),
+            dma((n_plane,)),
+            dma((n_plane,)),
+            dma((n_group,)),
+            dma((n_group,)),
+            dma((n_plane,)),
+            dma((n_plane,)),
+        ],
+        compiler_params=pltpu.CompilerParams(
+            collective_id=0, has_side_effects=True, vmem_limit_bytes=48 * 1024 * 1024
+        ),
+    )(
+        t_idx,
+        noise_gen.transpose(0, 2, 1),
+        noise_score.transpose(0, 2, 1),
+        prev_latents.transpose(0, 2, 1),
+        w_in[0],
+        w_qkv[0].transpose(1, 0, 2),
+        w_out[0].T,
+        w_final[0].T,
+        mod_scale,
+        mod_shift,
+        saved_features,
+    )
+    return prediction.transpose(0, 2, 1)[None], dmd_grad.transpose(0, 2, 1), grad.T
+
+
 def solution(mesh):
     placed = (
         P("dp", "seq", None),
@@ -113,7 +607,7 @@
         P("dp", "seq", None),
     )
     return jax.shard_map(
-        per_device,
+        functools.partial(per_device, dict(mesh.shape)),
         mesh=mesh,
         in_specs=placed,
         out_specs=(P("group", "dp", "seq", None), P("dp", "seq", None), P()),

time: 257 us -> 54.9 us (0.21)
  waiting for transfers between devices: 189 us -> 0 us
  Pallas kernels: 0 us -> 41.9 us
  matrix products: 32.2 us -> 0 us
  between operations: 13.9 us -> 0.66 us
  other arithmetic: 7.86 us -> 0 us
  blocking collectives: 7.14 us -> 0 us
  local copies, waits for them, and re-layouts: 4.35 us -> 11.2 us
    psum x2 -> x0, waiting for transfers between devices: 88.9 us -> none  [the longest x1 54.7 us: per_device(): total_grad = lax.psum(partial_grad, ('seq', 'dp'))]
    all_gather x1 -> x0, waiting for transfers between devices: 80.4 us -> none  [per_device(): lax.all_gather(features, 'seq', axis=1, tiled=True)]
    pallas_call x0 -> x1, Pallas kernels: none -> 41.9 us  [per_device(): pl.pallas_call(functools.partial(kernel, (n_group, n_seq, n_dp)), out_sha...]
    dot_general x5 -> x0, matrix products: 25 us -> none  [the longest x1 11.2 us: per_device(): jnp.einsum('ind,de->ine', lax.all_gather(features, 'seq', axis=1, tiled=T...]
    reduce_scatter x1 -> x0, waiting for transfers between devices: 19.7 us -> none  [per_device(): lax.psum_scatter(jnp.einsum('sca,af->scf', token_leading_layout, output_l...]
    sub x1 -> x0, matrix products: 7.14 us -> none  [per_device(): probs = jax.nn.softmax(scores, axis=-1).astype(jnp.bfloat16)]
    psum x1 -> x0, blocking collectives: 7.14 us -> none  [per_device(): total_dev = lax.psum(deviation, 'seq')]
    unnamed x17 -> x23, local copies, waits for them, and re-layouts: 4.35 us -> 11.2 us
  transfers between devices with their start and end apart: 4 -> 0, of which waited for: 4 -> 0; matrix products, arithmetic and copies ran while one was open for 2% -> 0% of each run, Pallas kernels for 0% -> 0%
where the time goes in v1:
time: 54.9 us; the launch traced here: 53.8 us
  Pallas kernels  41.9 us (76%)
  local copies, waits for them, and re-layouts  11.2 us (20%)
  between operations  0.66 us (1%)
    pallas_call x1, Pallas kernels, per_device(): pl.pallas_call(functools.partial(kernel, (n_group, n_seq, n_dp)), out_sha...  41.9 us
    unnamed x23, local copies, waits for them, and re-layouts  11.2 us

profile of v1, /device:TPU:1, one launch (start us, length us, event | category | flops | bytes accessed | tf_op | source)
XLA Modules:
  0.0 53.8 jit_solution(4952120359665813655)
XLA Ops:
  0.6 0.0 copy-start
  0.6 1.7 %copy-done = bf16[1,3072,3,128]{3,1,2,0:T(8,128)(2,1)S(1)} copy-done((bf16[1,3072,3,128]{3,1,2,0:T(8,128)(2,1)S(1)}, bf16[1,3072,3,128]{3,1,2,0:T(8,128)(2,1)}, u32[]{:S(2)}) %copy-start) | copy-done | bytes 2359320
  2.3 0.0 copy-start.1
  2.3 1.0 %copy-done.1 = bf16[1,64,3072]{2,1,0:T(8,128)(2,1)S(1)} copy-done((bf16[1,64,3072]{2,1,0:T(8,128)(2,1)S(1)}, bf16[1,64,3072]{2,1,0:T(8,128)(2,1)}, u32[]{:S(2)}) %copy-start.1) | copy-done | bytes 393240
  3.3 0.0 copy-start.2
  3.3 1.0 %copy-done.2 = bf16[1,3072,64]{1,2,0:T(8,128)(2,1)S(1)} copy-done((bf16[1,3072,64]{1,2,0:T(8,128)(2,1)S(1)}, bf16[1,3072,64]{1,2,0:T(8,128)(2,1)}, u32[]{:S(2)}) %copy-start.2) | copy-done | bytes 393240
  4.3 0.0 copy-start.3
  4.3 0.9 %copy-done.3 = f32[2,256,64]{1,2,0:T(8,128)S(1)} copy-done((f32[2,256,64]{1,2,0:T(8,128)S(1)}, f32[2,256,64]{1,2,0:T(8,128)}, u32[]{:S(2)}) %copy-start.3) | copy-done | bytes 131096
  5.2 0.0 copy-start.4
  5.2 0.8 %copy-done.4 = bf16[2,256,64]{1,2,0:T(8,128)(2,1)S(1)} copy-done((bf16[2,256,64]{1,2,0:T(8,128)(2,1)S(1)}, bf16[2,256,64]{1,2,0:T(8,128)(2,1)}, u32[]{:S(2)}) %copy-start.4) | copy-done | bytes 65560
  6.0 0.0 copy-start.5
  6.0 0.8 %copy-done.5 = bf16[2,256,64]{1,2,0:T(8,128)(2,1)S(1)} copy-done((bf16[2,256,64]{1,2,0:T(8,128)(2,1)S(1)}, bf16[2,256,64]{1,2,0:T(8,128)(2,1)}, u32[]{:S(2)}) %copy-start.5) | copy-done | bytes 65560
  6.9 0.0 copy-start.6
  6.9 0.7 %copy-done.6 = bf16[1,128,64]{1,2,0:T(8,128)(2,1)S(1)} copy-done((bf16[1,128,64]{1,2,0:T(8,128)(2,1)S(1)}, bf16[1,128,64]{1,2,0:T(8,128)(2,1)}, u32[]{:S(2)}) %copy-start.6) | copy-done | bytes 16408
  7.6 0.0 copy-start.7
  7.6 0.7 %copy-done.7 = f32[1,3072]{1,0:T(1,128)S(1)} copy-done((f32[1,3072]{1,0:T(1,128)S(1)}, f32[1,3072]{1,0:T(1,128)}, u32[]{:S(2)}) %copy-start.7) | copy-done | bytes 12312
  8.3 0.0 copy-start.8
  8.3 0.7 %copy-done.8 = f32[1,3072]{1,0:T(1,128)S(1)} copy-done((f32[1,3072]{1,0:T(1,128)S(1)}, f32[1,3072]{1,0:T(1,128)}, u32[]{:S(2)}) %copy-start.8) | copy-done | bytes 12312
  9.0 0.0 copy-start.9
  9.0 0.7 %copy-done.9 = s32[2]{0:T(128)S(1)} copy-done((s32[2]{0:T(128)S(1)}, s32[2]{0:T(128)}, u32[]{:S(2)}) %copy-start.9) | copy-done | bytes 32
  9.7 41.9 %shard_map.130 = (f32[2,64,256]{2,1,0:T(8,128)S(1)}, f32[2,64,256]{2,1,0:T(8,128)S(1)}, f32[64,3072]{1,0:T(8,128)S(1)}) custom-call(s32[2]{0:T(128)S(1)} %copy-done.9, bf16[2,64,256]{2,1,0:T(8,128)(2,1)S(1)} %bitcast.25, bf16[2,64,256]{2,1,0:T(8,128)(2,1)S(1)} %bitcast.26, f32[2,64,256]{2,1,0:T(8,128)S(1)} %bitcast.24, bf16[64,3072]{1,0:T(8,128)(2,1)S(1)} %bitcast.20, ...), custom_call_target="tpu_custom_call" | custom-call | tf_op jit(solution)/shard_map/pallas_call | solution.py:515
  51.6 0.7 %copy.17 = f32[1,2,256,64]{2,3,1,0:T(8,128)} copy(f32[1,2,256,64]{2,3,1,0:T(8,128)S(1)} %bitcast.23) | data formatting | bytes 262144
  52.3 0.7 %copy.18 = f32[2,256,64]{1,2,0:T(8,128)} copy(f32[2,256,64]{1,2,0:T(8,128)S(1)} %bitcast.22) | data formatting | bytes 262144
  52.9 0.9 %copy.19 = f32[3072,64]{0,1:T(8,128)} copy(f32[3072,64]{0,1:T(8,128)S(1)} %bitcast.19) | data formatting | bytes 1572864
Async XLA Ops:
  0.6 1.7 %copy-start = (bf16[1,3072,3,128]{3,1,2,0:T(8,128)(2,1)S(1)}, bf16[1,3072,3,128]{3,1,2,0:T(8,128)(2,1)}, u32[]{:S(2)}) copy-start(bf16[1,3072,3,128]{3,1,2,0:T(8,128)(2,1)} %param.16) | copy-start | bytes 7077892
  2.3 1.0 %copy-start.1 = (bf16[1,64,3072]{2,1,0:T(8,128)(2,1)S(1)}, bf16[1,64,3072]{2,1,0:T(8,128)(2,1)}, u32[]{:S(2)}) copy-start(bf16[1,64,3072]{2,1,0:T(8,128)(2,1)} %param.15) | copy-start | bytes 1179652
  3.3 1.0 %copy-start.2 = (bf16[1,3072,64]{1,2,0:T(8,128)(2,1)S(1)}, bf16[1,3072,64]{1,2,0:T(8,128)(2,1)}, u32[]{:S(2)}) copy-start(bf16[1,3072,64]{1,2,0:T(8,128)(2,1)} %param.18) | copy-start | bytes 1179652
  4.3 0.9 %copy-start.3 = (f32[2,256,64]{1,2,0:T(8,128)S(1)}, f32[2,256,64]{1,2,0:T(8,128)}, u32[]{:S(2)}) copy-start(f32[2,256,64]{1,2,0:T(8,128)} %param.13) | copy-start | bytes 393220
  5.2 0.8 %copy-start.4 = (bf16[2,256,64]{1,2,0:T(8,128)(2,1)S(1)}, bf16[2,256,64]{1,2,0:T(8,128)(2,1)}, u32[]{:S(2)}) copy-start(bf16[2,256,64]{1,2,0:T(8,128)(2,1)} %param.11) | copy-start | bytes 196612
  6.0 0.8 %copy-start.5 = (bf16[2,256,64]{1,2,0:T(8,128)(2,1)S(1)}, bf16[2,256,64]{1,2,0:T(8,128)(2,1)}, u32[]{:S(2)}) copy-start(bf16[2,256,64]{1,2,0:T(8,128)(2,1)} %param.12) | copy-start | bytes 196612
  6.9 0.7 %copy-start.6 = (bf16[1,128,64]{1,2,0:T(8,128)(2,1)S(1)}, bf16[1,128,64]{1,2,0:T(8,128)(2,1)}, u32[]{:S(2)}) copy-start(bf16[1,128,64]{1,2,0:T(8,128)(2,1)} %param.17) | copy-start | bytes 49156
  7.6 0.7 %copy-start.7 = (f32[1,3072]{1,0:T(1,128)S(1)}, f32[1,3072]{1,0:T(1,128)}, u32[]{:S(2)}) copy-start(f32[1,3072]{1,0:T(1,128)} %scale_ref.1) | copy-start | bytes 36868
  8.3 0.7 %copy-start.8 = (f32[1,3072]{1,0:T(1,128)S(1)}, f32[1,3072]{1,0:T(1,128)}, u32[]{:S(2)}) copy-start(f32[1,3072]{1,0:T(1,128)} %shift_ref.1) | copy-start | bytes 36868
  9.0 0.7 %copy-start.9 = (s32[2]{0:T(128)S(1)}, s32[2]{0:T(128)}, u32[]{:S(2)}) copy-start(s32[2]{0:T(128)} %t_ref.1) | copy-start | bytes 28

commit v2 on v1

--- a/solution.py
+++ b/solution.py
@@ -132,19 +132,26 @@
 def kernel(
     dims,
     t_ref,
+    noise_gen_hbm,
+    noise_score_hbm,
+    prev_hbm,
+    w_in_hbm,
+    w_qkv_hbm,
+    w_out_hbm,
+    w_final_hbm,
+    scale_hbm,
+    shift_hbm,
+    saved_hbm,
+    pred_ref,
+    dmd_ref,
+    grad_ref,
     noise_gen_ref,
     noise_score_ref,
     prev_ref,
     w_in_ref,
-    w_qkv_hbm,
     w_out_ref,
-    w_final_hbm,
     scale_ref,
     shift_ref,
-    saved_hbm,
-    pred_ref,
-    dmd_ref,
-    grad_ref,
     w_qkv,
     w_final,
     saved,
@@ -182,12 +189,14 @@
     up_send,
     up_recv,
     all_send,
+    core_send,
     all_recv,
 ):
     n_group, n_seq, n_dp = dims
     n_plane = n_seq * n_dp
     images, channels, toks = prev_ref.shape
     width = w_in_ref.shape[1]
+    n_same = n_plane // 2
     head = w_out_ref.shape[1]
     share = saved.shape[2]
     chunk = grad_in.shape[2]
@@ -198,13 +207,20 @@
     here = g * n_seq + s
     place = s * n_dp + d
 
-    loads = [
-        pltpu.make_async_copy(w_qkv_hbm, w_qkv, load_sem.at[0]),
-        pltpu.make_async_copy(w_final_hbm, w_final, load_sem.at[1]),
-        pltpu.make_async_copy(
-            saved_hbm.at[:, :, pl.ds(pl.multiple_of(g * share, 128), share)], saved, load_sem.at[2]
-        ),
+    saved_part = saved_hbm.at[:, :, pl.ds(pl.multiple_of(g * share, 128), share)]
+    pairs = [
+        (noise_gen_hbm, noise_gen_ref),
+        (noise_score_hbm, noise_score_ref),
+        (prev_hbm, prev_ref),
+        (w_in_hbm, w_in_ref),
+        (scale_hbm, scale_ref),
+        (shift_hbm, shift_ref),
+        (w_qkv_hbm, w_qkv),
+        (w_final_hbm, w_final),
+        (w_out_hbm, w_out_ref),
+        (saved_part, saved),
     ]
+    loads = [pltpu.make_async_copy(src, dst, load_sem.at[at]) for at, (src, dst) in enumerate(pairs)]
     for load in loads:
         load.start()
 
@@ -238,6 +254,8 @@
     def own_level(i, lanes):
         return generator + (1.0 - generator) * level(i, lanes)
 
+    for load in loads[:3]:
+        load.wait()
     for i in range(images):
         lv = level(i, toks)
         noisy[i] = (1.0 - lv) * prev_ref[i] + lv * noise_score_ref[i].astype(F32)
@@ -277,6 +295,8 @@
     for k in range(1, n_seq):
         send(xg.at[0], xg.at[k], x_send.at[k], x_recv.at[k], seq_peer(n_seq - k))
 
+    for load in loads[3:6]:
+        load.wait()
     both = jnp.concatenate([xg[0, i] for i in range(images)], axis=1)
     square = jnp.zeros((1, images * toks), F32)
     step = width // 4
@@ -303,8 +323,8 @@
         shift_rows = jnp.where(row == at, term.astype(F32), shift_rows)
     left[base : base + ROWS] = shift_rows.astype(BF16)
 
-    loads[0].wait()
-    loads[1].wait()
+    for load in loads[6:9]:
+        load.wait()
     maps = [dot(left[...], w_qkv[c]) for c in range(3)] + [dot_last(left[...], w_final[...])]
     maps = jnp.concatenate(maps, axis=1)
     total = 3 * head + channels
@@ -397,7 +417,7 @@
                     dev_recv.at[here],
                     {"group": lax.rem(g + dg, n_group), "seq": lax.rem(s + ds, n_seq)},
                 )
-    loads[2].wait()
+    loads[9].wait()
     for k in range(1, n_group):
         frm = lax.rem(g + k, n_group)
         theirs = diff.at[:, pl.ds(pl.multiple_of(frm * ROWS, ROWS), ROWS), :]
@@ -439,17 +459,39 @@
         summed = summed + grad_in[k].astype(F32)
     normalizer = 1.0 / math.sqrt(images * n_dp * n_seq * toks)
     gathered[place, g] = (summed * normalizer).astype(BF16)
+    other_core = {"seq": s + 1 - 2 * lax.rem(s, 2)}
+
+    def same_core(k):
+        seq, dp = lax.rem(s + 2 * (k // n_dp), n_seq), lax.rem(d + k % n_dp, n_dp)
+        return seq * n_dp + dp, {"seq": seq, "dp": dp}
+
+    def pass_on(h, turn):
+        for k in range(1, n_same):
+            at = gathered.at[place, h]
+            send(at, at, all_send.at[k, turn], all_recv.at[place, h], same_core(k)[1])
+        at = gathered.at[place, h]
+        send(at, at, core_send.at[0, turn], all_recv.at[place, h], other_core)
+
     for k in range(1, n_group):
-        send(gathered.at[place, g], gathered.at[place, g], up_send.at[k], up_recv.at[g], group_peer(k))
+        at = gathered.at[place, g]
+        send(at, at, up_send.at[k], up_recv.at[g], group_peer(k))
+    pass_on(g, 0)
     for k in range(1, n_group):
         frm = lax.rem(g + k, n_group)
         arrive(gathered.at[place, frm], up_send.at[k], up_recv.at[frm], group_peer(k))
-    for k in range(1, n_plane):
-        to, device = plane_peer(k)
-        send(gathered.at[place], gathered.at[place], all_send.at[k], all_recv.at[place], device)
-    for k in range(1, n_plane):
-        frm, device = plane_peer(k)
-        arrive(gathered.at[frm], all_send.at[k], all_recv.at[frm], device)
+        pass_on(frm, k)
+    for turn in range(n_group):
+        h = lax.rem(g + turn, n_group)
+        for k in range(1, n_same):
+            frm, device = same_core(k)
+            at = gathered.at[frm, h]
+            arrive(at, all_send.at[k, turn], all_recv.at[frm, h], device)
+            send(at, at, core_send.at[k, turn], all_recv.at[frm, h], other_core)
+    for turn in range(n_group):
+        h = lax.rem(g + turn, n_group)
+        for k in range(n_same):
+            frm = same_core(k)[0] + n_dp - 2 * n_dp * lax.rem(s, 2)
+            arrive(gathered.at[frm, h], core_send.at[k, turn], all_recv.at[frm, h], other_core)
     for o in range(n_plane):
         r0 = (o // lane_blocks) * ROWS
         for h in range(n_group):
@@ -468,6 +510,7 @@
         and images <= 8
         and toks % 128 == 0
         and head % 128 == 0
+        and shape["seq"] % 2 == 0
         and n_plane % row_blocks == 0
         and width % (n_group * (n_plane // row_blocks) * 128) == 0
     )
@@ -508,7 +551,7 @@
     share = width // n_group
     chunk = share // (n_plane // (channels // ROWS))
     vmem = pl.BlockSpec(memory_space=pltpu.VMEM)
-    anywhere = pl.BlockSpec(memory_space=pl.ANY)
+    hbm = pl.BlockSpec(memory_space=pltpu.HBM)
     dma = pltpu.SemaphoreType.DMA
     all_tokens = n_seq * toks
     total_in = n_group * n_seq
@@ -519,21 +562,16 @@
             jax.ShapeDtypeStruct((images, channels, toks), F32),
             jax.ShapeDtypeStruct((channels, width), F32),
         ),
-        in_specs=[
-            pl.BlockSpec(memory_space=pltpu.SMEM),
-            vmem,
-            vmem,
-            vmem,
-            vmem,
-            anywhere,
-            vmem,
-            anywhere,
-            vmem,
-            vmem,
-            anywhere,
-        ],
+        in_specs=[pl.BlockSpec(memory_space=pltpu.SMEM)] + [hbm] * 10,
         out_specs=(vmem, vmem, vmem),
         scratch_shapes=[
+            pltpu.VMEM((images, channels, toks), BF16),
+            pltpu.VMEM((images, channels, toks), BF16),
+            pltpu.VMEM((images, channels, toks), F32),
+            pltpu.VMEM((channels, width), BF16),
+            pltpu.VMEM((channels, head), BF16),
+            pltpu.VMEM((1, width), F32),
+            pltpu.VMEM((1, width), F32),
             pltpu.VMEM((3, width, head), BF16),
             pltpu.VMEM((channels, width), BF16),
             pltpu.VMEM((images, toks, share), BF16),
@@ -553,7 +591,7 @@
             pltpu.VMEM((n_plane, ROWS, chunk), BF16),
             pltpu.VMEM((n_plane, ROWS, chunk), BF16),
             pltpu.VMEM((n_plane, n_group, ROWS, chunk), BF16),
-            dma((3,)),
+            dma((10,)),
             dma((n_seq,)),
             dma((n_seq,)),
             dma((n_seq,)),
@@ -570,11 +608,12 @@
             dma((n_plane,)),
             dma((n_group,)),
             dma((n_group,)),
-            dma((n_plane,)),
-            dma((n_plane,)),
+            dma((n_plane // 2, n_group)),
+            dma((n_plane // 2, n_group)),
+            dma((n_plane, n_group)),
         ],
         compiler_params=pltpu.CompilerParams(
-            collective_id=0, has_side_effects=True, vmem_limit_bytes=48 * 1024 * 1024
+            collective_id=0, has_side_effects=True, vmem_limit_bytes=60 * 1024 * 1024
         ),
     )(
         t_idx,

time: 54.9 us -> 48.2 us (0.88); the launches traced: 53.8 us -> 48 us
  local copies, waits for them, and re-layouts: 11.2 us -> 5.2 us
    unnamed x23 -> x3, local copies, waits for them, and re-layouts: 11.2 us -> 5.2 us
where the time goes in v2:
time: 48.2 us; the launch traced here: 48 us
  Pallas kernels  42.1 us (87%)
  local copies, waits for them, and re-layouts  5.2 us (11%)
  between operations  0.64 us (1%)
    pallas_call x1, Pallas kernels, per_device(): pl.pallas_call(functools.partial(kernel, (n_group, n_seq, n_dp)), out_sha...  42.1 us
    unnamed x3, local copies, waits for them, and re-layouts  5.2 us

profile of v2, /device:TPU:1, one launch (start us, length us, event | category | flops | bytes accessed | tf_op | source)
XLA Modules:
  0.0 48.0 jit_solution(15100927708098951051)
XLA Ops:
  0.6 42.1 %shard_map.130 = (f32[2,64,256]{2,1,0:T(8,128)}, f32[2,64,256]{2,1,0:T(8,128)}, f32[64,3072]{1,0:T(8,128)}) custom-call(s32[2]{0:T(128)} %t_ref.1, bf16[2,64,256]{2,1,0:T(8,128)(2,1)} %bitcast.25, bf16[2,64,256]{2,1,0:T(8,128)(2,1)} %bitcast.26, f32[2,64,256]{2,1,0:T(8,128)} %bitcast.24, bf16[64,3072]{1,0:T(8,128)(2,1)} %bitcast.20, ...), custom_call_target="tpu_custom_call" | custom-call | tf_op jit(solution)/shard_map/pallas_call | solution.py:558
  42.8 1.6 %copy.17 = f32[1,2,256,64]{2,3,1,0:T(8,128)} copy(f32[1,2,256,64]{2,3,1,0:T(8,128)} %bitcast.23) | data formatting | bytes 262144
  44.3 1.6 %copy.18 = f32[2,256,64]{1,2,0:T(8,128)} copy(f32[2,256,64]{1,2,0:T(8,128)} %bitcast.22) | data formatting | bytes 262144
  45.9 2.1 %copy.19 = f32[3072,64]{0,1:T(8,128)} copy(f32[3072,64]{0,1:T(8,128)} %bitcast.19) | data formatting | bytes 1572864

commit v3 on v2

--- a/solution.py
+++ b/solution.py
@@ -131,7 +131,7 @@
 
 def kernel(
     dims,
-    t_ref,
+    t_hbm,
     noise_gen_hbm,
     noise_score_hbm,
     prev_hbm,
@@ -152,6 +152,7 @@
     w_out_ref,
     scale_ref,
     shift_ref,
+    t_ref,
     w_qkv,
     w_final,
     saved,
@@ -198,16 +199,13 @@
     width = w_in_ref.shape[1]
     n_same = n_plane // 2
     head = w_out_ref.shape[1]
-    share = saved.shape[2]
-    chunk = grad_in.shape[2]
-    lane_blocks = share // chunk
+    chunk = grad_in.shape[3]
     g = lax.axis_index("group")
     s = lax.axis_index("seq")
     d = lax.axis_index("dp")
-    here = g * n_seq + s
     place = s * n_dp + d
-
-    saved_part = saved_hbm.at[:, :, pl.ds(pl.multiple_of(g * share, 128), share)]
+    here = g * n_plane + place
+
     pairs = [
         (noise_gen_hbm, noise_gen_ref),
         (noise_score_hbm, noise_score_ref),
@@ -215,36 +213,30 @@
         (w_in_hbm, w_in_ref),
         (scale_hbm, scale_ref),
         (shift_hbm, shift_ref),
-        (w_qkv_hbm, w_qkv),
         (w_final_hbm, w_final),
         (w_out_hbm, w_out_ref),
-        (saved_part, saved),
     ]
+    pairs += [(w_qkv_hbm.at[c], w_qkv.at[:, c * head : (c + 1) * head]) for c in range(3)]
+    pairs += [(saved_hbm, saved), (t_hbm, t_ref)]
     loads = [pltpu.make_async_copy(src, dst, load_sem.at[at]) for at, (src, dst) in enumerate(pairs)]
     for load in loads:
         load.start()
 
     barrier = pltpu.get_barrier_semaphore()
-    peers = 0
-    for dg in range(n_group):
-        for ds in range(n_seq):
-            if dg or ds:
-                pl.semaphore_signal(
-                    barrier,
-                    inc=1,
-                    device_id={"group": lax.rem(g + dg, n_group), "seq": lax.rem(s + ds, n_seq)},
-                    device_id_type=MESH,
-                )
-                peers += 1
-    for ds in range(n_seq):
-        for dd in range(1, n_dp):
-            pl.semaphore_signal(
-                barrier,
-                inc=1,
-                device_id={"seq": lax.rem(s + ds, n_seq), "dp": lax.rem(d + dd, n_dp)},
-                device_id_type=MESH,
-            )
-            peers += 1
+    others = [
+        (dg, ds, dd)
+        for dg in range(n_group)
+        for ds in range(n_seq)
+        for dd in range(n_dp)
+        if dg or ds or dd
+    ]
+
+    def other(dg, ds, dd):
+        gg, ss, dp = lax.rem(g + dg, n_group), lax.rem(s + ds, n_seq), lax.rem(d + dd, n_dp)
+        return (gg * n_seq + ss) * n_dp + dp, {"group": gg, "seq": ss, "dp": dp}
+
+    for shift in others:
+        pl.semaphore_signal(barrier, inc=1, device_id=other(*shift)[1], device_id_type=MESH)
 
     generator = jnp.where(g == 0, 1.0, 0.0).astype(F32)
 
@@ -254,7 +246,7 @@
     def own_level(i, lanes):
         return generator + (1.0 - generator) * level(i, lanes)
 
-    for load in loads[:3]:
+    for load in loads[:3] + loads[12:]:
         load.wait()
     for i in range(images):
         lv = level(i, toks)
@@ -263,7 +255,7 @@
         pred_ref[i] = model_input
         xg[0, i] = model_input.astype(BF16)
 
-    pl.semaphore_wait(barrier, peers)
+    pl.semaphore_wait(barrier, len(others))
 
     sends = []
 
@@ -323,10 +315,9 @@
         shift_rows = jnp.where(row == at, term.astype(F32), shift_rows)
     left[base : base + ROWS] = shift_rows.astype(BF16)
 
-    for load in loads[6:9]:
+    for load in loads[6:11]:
         load.wait()
-    maps = [dot(left[...], w_qkv[c]) for c in range(3)] + [dot_last(left[...], w_final[...])]
-    maps = jnp.concatenate(maps, axis=1)
+    maps = jnp.concatenate([dot(left[...], w_qkv[...]), dot_last(left[...], w_final[...])], axis=1)
     total = 3 * head + channels
     plain = maps[0:channels]
     per_level = sum(maps[(at + 1) * channels : (at + 2) * channels] for at in range(PARTS))
@@ -395,7 +386,7 @@
         arrive(split_in.at[frm], split_send.at[k], split_recv.at[frm], group_peer(k))
 
     part = pl.ds(pl.multiple_of(g * ROWS, ROWS), ROWS)
-    sums = []
+    sums, mine = [], []
     for i in range(images):
         lv = level(i, toks)
         guided = 2.5 * split_in[1, i].astype(F32) - 1.5 * split_in[2, i].astype(F32)
@@ -403,48 +394,16 @@
         away = jnp.abs(prev_ref[i, part, :] - real)
         away = jnp.sum(jnp.sum(away, axis=0, keepdims=True), axis=1, keepdims=True)
         sums.append(jnp.broadcast_to(away, (1, 128)))
-        diff[i, part, :] = (lv * (guided - split_in[3, i].astype(F32))).astype(BF16)
+        mine.append((lv * (guided - split_in[3, i].astype(F32))).astype(BF16))
+        diff[i, part, :] = mine[i]
     dev[here] = jnp.concatenate(sums + [jnp.zeros((8 - images, 128), F32)], axis=0)
-    for k in range(1, n_group):
-        send(diff.at[:, part, :], diff.at[:, part, :], diff_send.at[k], diff_recv.at[g], group_peer(k))
-    for dg in range(n_group):
-        for ds in range(n_seq):
-            if dg or ds:
-                send(
-                    dev.at[here],
-                    dev.at[here],
-                    dev_send.at[dg * n_seq + ds],
-                    dev_recv.at[here],
-                    {"group": lax.rem(g + dg, n_group), "seq": lax.rem(s + ds, n_seq)},
-                )
-    loads[9].wait()
-    for k in range(1, n_group):
-        frm = lax.rem(g + k, n_group)
-        theirs = diff.at[:, pl.ds(pl.multiple_of(frm * ROWS, ROWS), ROWS), :]
-        arrive(theirs, diff_send.at[k], diff_recv.at[frm], group_peer(k))
-    products = [dot(diff[i], saved[i]) for i in range(images)]
-    for dg in range(n_group):
-        for ds in range(n_seq):
-            if dg or ds:
-                there = lax.rem(g + dg, n_group) * n_seq + lax.rem(s + ds, n_seq)
-                arrive(
-                    dev.at[there],
-                    dev_send.at[dg * n_seq + ds],
-                    dev_recv.at[there],
-                    {"group": lax.rem(g + dg, n_group), "seq": lax.rem(s + ds, n_seq)},
-                )
-    away = dev[0]
-    for at in range(1, n_group * n_seq):
-        away = away + dev[at]
-    spread = away * (1.0 / (n_seq * toks * channels)) + 1e-05
-    gradient = 0.0
+    for at, shift in enumerate(others):
+        send(dev.at[here], dev.at[here], dev_send.at[at], dev_recv.at[here], other(*shift)[1])
+    loads[11].wait()
     for i in range(images):
-        over = 1.0 / spread[i : i + 1, 0:1]
-        gradient = gradient - products[i] * over
-        dmd_ref[i] = diff[i].astype(F32) * over
-    for o in range(n_plane):
-        r0, c0 = (o // lane_blocks) * ROWS, (o % lane_blocks) * chunk
-        grad_out[o] = gradient[r0 : r0 + ROWS, c0 : c0 + chunk].astype(BF16)
+        product = dot(mine[i], saved[i])
+        for o in range(n_plane):
+            grad_out[o, i] = product[:, o * chunk : (o + 1) * chunk].astype(BF16)
 
     def plane_peer(k):
         to = lax.rem(place + k, n_plane)
@@ -452,13 +411,30 @@
 
     for k in range(1, n_plane):
         to, device = plane_peer(k)
-        send(grad_out.at[to], grad_in.at[k], grad_send.at[k], grad_recv.at[k], device)
-    summed = grad_out[place].astype(F32)
+        send(grad_out.at[to], grad_in.at[place], grad_send.at[k], grad_recv.at[place], device)
+    grad_in[place] = grad_out[place]
+    for k in range(1, n_group):
+        at = diff.at[:, part, :]
+        send(at, at, diff_send.at[k], diff_recv.at[g], group_peer(k))
+    for at, shift in enumerate(others):
+        there, device = other(*shift)
+        arrive(dev.at[there], dev_send.at[at], dev_recv.at[there], device)
+    over = []
+    for dd in range(n_dp):
+        away = dev[dd]
+        for at in range(1, n_group * n_seq):
+            away = away + dev[at * n_dp + dd]
+        over.append(1.0 / (away * (1.0 / (n_seq * toks * channels)) + 1e-05))
     for k in range(1, n_plane):
-        arrive(grad_in.at[k], grad_send.at[k], grad_recv.at[k], plane_peer(n_plane - k)[1])
-        summed = summed + grad_in[k].astype(F32)
+        frm, device = plane_peer(k)
+        arrive(grad_in.at[frm], grad_send.at[k], grad_recv.at[frm], device)
     normalizer = 1.0 / math.sqrt(images * n_dp * n_seq * toks)
-    gathered[place, g] = (summed * normalizer).astype(BF16)
+    summed = jnp.zeros((ROWS, chunk), F32)
+    for o in range(n_plane):
+        for i in range(images):
+            weight = over[o % n_dp][i : i + 1, 0:1] * -normalizer
+            summed = summed + grad_in[o, i].astype(F32) * weight
+    gathered[place, g] = summed.astype(BF16)
     other_core = {"seq": s + 1 - 2 * lax.rem(s, 2)}
 
     def same_core(k):
@@ -480,6 +456,15 @@
         frm = lax.rem(g + k, n_group)
         arrive(gathered.at[place, frm], up_send.at[k], up_recv.at[frm], group_peer(k))
         pass_on(frm, k)
+    for k in range(1, n_group):
+        frm = lax.rem(g + k, n_group)
+        at = diff.at[:, pl.ds(pl.multiple_of(frm * ROWS, ROWS), ROWS), :]
+        arrive(at, diff_send.at[k], diff_recv.at[frm], group_peer(k))
+    own_over = over[0]
+    for dd in range(1, n_dp):
+        own_over = jnp.where(d == dd, over[dd], own_over)
+    for i in range(images):
+        dmd_ref[i] = diff[i].astype(F32) * own_over[i : i + 1, 0:1]
     for turn in range(n_group):
         h = lax.rem(g + turn, n_group)
         for k in range(1, n_same):
@@ -493,17 +478,15 @@
             frm = same_core(k)[0] + n_dp - 2 * n_dp * lax.rem(s, 2)
             arrive(gathered.at[frm, h], core_send.at[k, turn], all_recv.at[frm, h], other_core)
     for o in range(n_plane):
-        r0 = (o // lane_blocks) * ROWS
         for h in range(n_group):
-            c0 = h * share + (o % lane_blocks) * chunk
-            grad_ref[r0 : r0 + ROWS, c0 : c0 + chunk] = gathered[o, h].astype(F32)
+            at = (slice(h * ROWS, (h + 1) * ROWS), slice(o * chunk, (o + 1) * chunk))
+            grad_ref[at] = gathered[o, h].astype(F32)
     for copy in sends:
         copy.wait_send()
 
 
 def fits(shape, images, toks, channels, width, head):
     n_group, n_plane = shape["group"], shape["seq"] * shape["dp"]
-    row_blocks = channels // ROWS
     return (
         n_group == 4
         and channels == n_group * ROWS
@@ -511,8 +494,7 @@
         and toks % 128 == 0
         and head % 128 == 0
         and shape["seq"] % 2 == 0
-        and n_plane % row_blocks == 0
-        and width % (n_group * (n_plane // row_blocks) * 128) == 0
+        and width % (n_plane * 128) == 0
     )
 
 
@@ -548,13 +530,12 @@
         )
     n_group, n_seq, n_dp = shape["group"], shape["seq"], shape["dp"]
     n_plane = n_seq * n_dp
-    share = width // n_group
-    chunk = share // (n_plane // (channels // ROWS))
+    chunk = width // n_plane
     vmem = pl.BlockSpec(memory_space=pltpu.VMEM)
     hbm = pl.BlockSpec(memory_space=pltpu.HBM)
     dma = pltpu.SemaphoreType.DMA
     all_tokens = n_seq * toks
-    total_in = n_group * n_seq
+    total_in = n_group * n_plane
     prediction, dmd_grad, grad = pl.pallas_call(
         functools.partial(kernel, (n_group, n_seq, n_dp)),
         out_shape=(
@@ -562,7 +543,7 @@
             jax.ShapeDtypeStruct((images, channels, toks), F32),
             jax.ShapeDtypeStruct((channels, width), F32),
         ),
-        in_specs=[pl.BlockSpec(memory_space=pltpu.SMEM)] + [hbm] * 10,
+        in_specs=[hbm] * 11,
         out_specs=(vmem, vmem, vmem),
         scratch_shapes=[
             pltpu.VMEM((images, channels, toks), BF16),
@@ -572,9 +553,10 @@
             pltpu.VMEM((channels, head), BF16),
             pltpu.VMEM((1, width), F32),
             pltpu.VMEM((1, width), F32),
-            pltpu.VMEM((3, width, head), BF16),
+            pltpu.SMEM((images,), jnp.int32),
+            pltpu.VMEM((width, 3 * head), BF16),
             pltpu.VMEM((channels, width), BF16),
-            pltpu.VMEM((images, toks, share), BF16),
+            pltpu.VMEM((images, toks, width), BF16),
             pltpu.VMEM(((PARTS + 1) * channels + ROWS, width), BF16),
             pltpu.VMEM((n_seq, images, channels, toks), BF16),
             pltpu.VMEM((n_seq, 8, toks), F32),
@@ -588,10 +570,10 @@
             pltpu.VMEM((n_group, images, ROWS, toks), BF16),
             pltpu.VMEM((images, channels, toks), BF16),
             pltpu.VMEM((total_in, 8, 128), F32),
-            pltpu.VMEM((n_plane, ROWS, chunk), BF16),
-            pltpu.VMEM((n_plane, ROWS, chunk), BF16),
+            pltpu.VMEM((n_plane, images, ROWS, chunk), BF16),
+            pltpu.VMEM((n_plane, images, ROWS, chunk), BF16),
             pltpu.VMEM((n_plane, n_group, ROWS, chunk), BF16),
-            dma((10,)),
+            dma((13,)),
             dma((n_seq,)),
             dma((n_seq,)),
             dma((n_seq,)),
@@ -613,20 +595,25 @@
             dma((n_plane, n_group)),
         ],
         compiler_params=pltpu.CompilerParams(
-            collective_id=0, has_side_effects=True, vmem_limit_bytes=60 * 1024 * 1024
+            collective_id=0, has_side_effects=True, vmem_limit_bytes=48 * 1024 * 1024
         ),
     )(
-        t_idx,
-        noise_gen.transpose(0, 2, 1),
-        noise_score.transpose(0, 2, 1),
-        prev_latents.transpose(0, 2, 1),
-        w_in[0],
-        w_qkv[0].transpose(1, 0, 2),
-        w_out[0].T,
-        w_final[0].T,
-        mod_scale,
-        mod_shift,
-        saved_features,
+        *(
+            pltpu.with_memory_space_constraint(x, pltpu.HBM)
+            for x in (
+                t_idx,
+                noise_gen.transpose(0, 2, 1),
+                noise_score.transpose(0, 2, 1),
+                prev_latents.transpose(0, 2, 1),
+                w_in[0],
+                w_qkv[0].transpose(1, 0, 2),
+                w_out[0].T,
+                w_final[0].T,
+                mod_scale,
+                mod_shift,
+                saved_features,
+            )
+        ),
     )
     return prediction.transpose(0, 2, 1)[None], dmd_grad.transpose(0, 2, 1), grad.T
 

time: 48.2 us -> 42.9 us (0.89)
  local copies, waits for them, and re-layouts: 5.2 us -> 2.19 us
  Pallas kernels: 42.1 us -> 39.9 us
    unnamed x3, local copies, waits for them, and re-layouts: 5.2 us -> 2.19 us
    pallas_call x1, Pallas kernels: 42.1 us -> 39.9 us  [per_device(): pl.pallas_call(functools.partial(kernel, (n_group, n_seq, n_dp)), out_sha...]
where the time goes in v3:
time: 42.9 us; the launch traced here: 42.7 us
  Pallas kernels  39.9 us (93%)
  local copies, waits for them, and re-layouts  2.19 us (5%)
  between operations  0.64 us (1%)
    pallas_call x1, Pallas kernels, per_device(): pl.pallas_call(functools.partial(kernel, (n_group, n_seq, n_dp)), out_sha...  39.9 us
    unnamed x3, local copies, waits for them, and re-layouts  2.19 us

profile of v3, /device:TPU:1, one launch (start us, length us, event | category | flops | bytes accessed | tf_op | source)
XLA Modules:
  0.0 42.7 jit_solution(17176755195249310503)
XLA Ops:
  0.6 39.9 %shard_map.130 = (f32[2,64,256]{2,1,0:T(8,128)S(1)}, f32[2,64,256]{2,1,0:T(8,128)S(1)}, f32[64,3072]{1,0:T(8,128)S(1)}) custom-call(s32[2]{0:T(128)} %t_hbm.1, bf16[2,64,256]{2,1,0:T(8,128)(2,1)} %bitcast.25, bf16[2,64,256]{2,1,0:T(8,128)(2,1)} %bitcast.26, f32[2,64,256]{2,1,0:T(8,128)} %bitcast.24, bf16[64,3072]{1,0:T(8,128)(2,1)} %bitcast.22, ...), custom_call_target="tpu_custom_call" | custom-call | tf_op jit(solution)/shard_map/pallas_call | solution.py:539
  40.5 0.7 %copy.17 = f32[1,2,256,64]{2,3,1,0:T(8,128)} copy(f32[1,2,256,64]{2,3,1,0:T(8,128)S(1)} %bitcast.20) | data formatting | bytes 262144
  41.2 0.7 %copy.18 = f32[2,256,64]{1,2,0:T(8,128)} copy(f32[2,256,64]{1,2,0:T(8,128)S(1)} %bitcast.19) | data formatting | bytes 262144
  41.8 0.9 %copy.19 = f32[3072,64]{0,1:T(8,128)} copy(f32[3072,64]{0,1:T(8,128)S(1)} %bitcast.18) | data formatting | bytes 1572864

commit v4 on v3

--- a/solution.py
+++ b/solution.py
@@ -328,7 +328,7 @@
         bias_rows = jnp.where(row == at, term.astype(F32), bias_rows)
     bias = dot_first(bias_rows.astype(BF16), jnp.ones((ROWS, toks), BF16))
     combined = [
-        jnp.concatenate(split_parts(plain + own_level(i, total) * per_level), axis=0)
+        jnp.concatenate(split_parts((plain + own_level(i, total) * per_level).T), axis=1)
         for i in range(images)
     ]
 
@@ -342,7 +342,7 @@
         for i in range(images):
             x = xg[k, i]
             stacked = jnp.concatenate([x] * PARTS, axis=0)
-            triple = dot_first(combined[i][:, :rows], stacked) * rg[k, i : i + 1, :] + bias[:rows]
+            triple = dot(combined[i][:rows], stacked) * rg[k, i : i + 1, :] + bias[:rows]
             queries[i, k] = (triple[:head] * factor).astype(BF16)
             keys[i, k * toks : (k + 1) * toks] = triple[head : 2 * head].T.astype(BF16)
             values[i, :, k * toks : (k + 1) * toks] = triple[2 * head : 3 * head].astype(BF16)
@@ -350,6 +350,14 @@
                 local.append(triple[3 * head :])
 
     own = []
+    def group_peer(k):
+        return {"group": lax.rem(g + k, n_group)}
+
+    def part_rows(h):
+        return pl.ds(pl.multiple_of(h * ROWS, ROWS), ROWS)
+
+    for k in range(1, n_seq):
+        split_in[g, k] = jnp.zeros((images, ROWS, toks), BF16)
     for k in list(range(1, n_seq)) + [0]:
         for i in range(images):
             scores = dot(keys[i], queries[i, k])
@@ -357,44 +365,51 @@
             norm = 1.0 / jnp.sum(weights, axis=0, keepdims=True)
             attended = (dot(values[i], weights.astype(BF16)) * norm).astype(BF16)
             term = dot(w_out_ref[...], attended)
-            if k:
-                vel_out[k, i] = term.astype(BF16)
-            else:
+            if k == 0:
+                term = term + local[i]
                 own.append(term)
+            vel_out[k, i] = term.astype(BF16)
+        for dg in range(1, n_group):
+            h = lax.rem(g + dg, n_group)
+            send(
+                vel_out.at[k, :, part_rows(h), :],
+                split_in.at[g, k],
+                split_send.at[dg, k],
+                split_recv.at[g, k],
+                {"group": h, "seq": lax.rem(s + k, n_seq)},
+            )
         if k:
             send(vel_out.at[k], vel_in.at[k], vel_send.at[k], vel_recv.at[k], seq_peer(k))
 
     for k in range(1, n_seq):
         arrive(vel_in.at[k], vel_send.at[k], vel_recv.at[k], seq_peer(n_seq - k))
     for i in range(images):
-        velocity = local[i] + own[i]
+        velocity = own[i]
         for k in range(1, n_seq):
             velocity = velocity + vel_in[k, i].astype(F32)
         pred_ref[i] = pred_ref[i] - own_level(i, toks) * velocity
         for h in range(n_group):
             split_out[h, i] = velocity[h * ROWS : (h + 1) * ROWS].astype(BF16)
-
-    def group_peer(k):
-        return {"group": lax.rem(g + k, n_group)}
-
-    for k in range(1, n_group):
-        to = lax.rem(g + k, n_group)
-        send(split_out.at[to], split_in.at[g], split_send.at[k], split_recv.at[g], group_peer(k))
-    split_in[g] = split_out[g]
-    for k in range(1, n_group):
-        frm = lax.rem(g + k, n_group)
-        arrive(split_in.at[frm], split_send.at[k], split_recv.at[frm], group_peer(k))
-
-    part = pl.ds(pl.multiple_of(g * ROWS, ROWS), ROWS)
+    split_in[g, 0] = split_out[g]
+    for dg in range(1, n_group):
+        frm = lax.rem(g + dg, n_group)
+        for k in range(n_seq):
+            device = {"group": frm, "seq": lax.rem(s + n_seq - k, n_seq)}
+            arrive(split_in.at[frm, k], split_send.at[dg, k], split_recv.at[frm, k], device)
+
+    def model_velocity(h, i):
+        return sum(split_in[h, k, i].astype(F32) for k in range(n_seq))
+
+    part = part_rows(g)
     sums, mine = [], []
     for i in range(images):
         lv = level(i, toks)
-        guided = 2.5 * split_in[1, i].astype(F32) - 1.5 * split_in[2, i].astype(F32)
+        guided = 2.5 * model_velocity(1, i) - 1.5 * model_velocity(2, i)
         real = noisy[i, part, :] - lv * guided
         away = jnp.abs(prev_ref[i, part, :] - real)
         away = jnp.sum(jnp.sum(away, axis=0, keepdims=True), axis=1, keepdims=True)
         sums.append(jnp.broadcast_to(away, (1, 128)))
-        mine.append((lv * (guided - split_in[3, i].astype(F32))).astype(BF16))
+        mine.append((lv * (guided - model_velocity(3, i))).astype(BF16))
         diff[i, part, :] = mine[i]
     dev[here] = jnp.concatenate(sums + [jnp.zeros((8 - images, 128), F32)], axis=0)
     for at, shift in enumerate(others):
@@ -567,7 +582,7 @@
             pltpu.VMEM((n_seq, images, channels, toks), BF16),
             pltpu.VMEM((n_seq, images, channels, toks), BF16),
             pltpu.VMEM((n_group, images, ROWS, toks), BF16),
-            pltpu.VMEM((n_group, images, ROWS, toks), BF16),
+            pltpu.VMEM((n_group, n_seq, images, ROWS, toks), BF16),
             pltpu.VMEM((images, channels, toks), BF16),
             pltpu.VMEM((total_in, 8, 128), F32),
             pltpu.VMEM((n_plane, images, ROWS, chunk), BF16),
@@ -580,8 +595,8 @@
             dma((n_seq,)),
             dma((n_seq,)),
             dma((n_seq,)),
-            dma((n_group,)),
-            dma((n_group,)),
+            dma((n_group, n_seq)),
+            dma((n_group, n_seq)),
             dma((n_group,)),
             dma((n_group,)),
             dma((total_in,)),

time: 42.9 us -> 41.9 us (0.977)
  Pallas kernels: 39.9 us -> 39 us
    pallas_call x1, Pallas kernels: 39.9 us -> 39 us  [per_device(): pl.pallas_call(functools.partial(kernel, (n_group, n_seq, n_dp)), out_sha...]
where the time goes in v4:
time: 41.9 us; the launch traced here: 41.8 us
  Pallas kernels  39 us (93%)
  local copies, waits for them, and re-layouts  2.19 us (5%)
  between operations  0.64 us (2%)
    pallas_call x1, Pallas kernels, per_device(): pl.pallas_call(functools.partial(kernel, (n_group, n_seq, n_dp)), out_sha...  39 us
    unnamed x3, local copies, waits for them, and re-layouts  2.19 us

profile of v4, /device:TPU:1, one launch (start us, length us, event | category | flops | bytes accessed | tf_op | source)
XLA Modules:
  0.0 41.8 jit_solution(2814694356688836175)
XLA Ops:
  0.6 39.0 %shard_map.130 = (f32[2,64,256]{2,1,0:T(8,128)S(1)}, f32[2,64,256]{2,1,0:T(8,128)S(1)}, f32[64,3072]{1,0:T(8,128)S(1)}) custom-call(s32[2]{0:T(128)} %t_hbm.1, bf16[2,64,256]{2,1,0:T(8,128)(2,1)} %bitcast.25, bf16[2,64,256]{2,1,0:T(8,128)(2,1)} %bitcast.26, f32[2,64,256]{2,1,0:T(8,128)} %bitcast.24, bf16[64,3072]{1,0:T(8,128)(2,1)} %bitcast.22, ...), custom_call_target="tpu_custom_call" | custom-call | tf_op jit(solution)/shard_map/pallas_call | solution.py:554
  39.6 0.7 %copy.17 = f32[1,2,256,64]{2,3,1,0:T(8,128)} copy(f32[1,2,256,64]{2,3,1,0:T(8,128)S(1)} %bitcast.20) | data formatting | bytes 262144
  40.3 0.7 %copy.18 = f32[2,256,64]{1,2,0:T(8,128)} copy(f32[2,256,64]{1,2,0:T(8,128)S(1)} %bitcast.19) | data formatting | bytes 262144
  40.9 0.9 %copy.19 = f32[3072,64]{0,1:T(8,128)} copy(f32[3072,64]{0,1:T(8,128)S(1)} %bitcast.18) | data formatting | bytes 1572864

commit v5 on v4

--- a/solution.py
+++ b/solution.py
@@ -255,38 +255,6 @@
         pred_ref[i] = model_input
         xg[0, i] = model_input.astype(BF16)
 
-    pl.semaphore_wait(barrier, len(others))
-
-    sends = []
-
-    def send(src, dst, send_sem, recv_sem, device):
-        copy = pltpu.make_async_remote_copy(
-            src_ref=src,
-            dst_ref=dst,
-            send_sem=send_sem,
-            recv_sem=recv_sem,
-            device_id=device,
-            device_id_type=MESH,
-        )
-        copy.start()
-        sends.append(copy)
-
-    def arrive(dst, send_sem, recv_sem, device):
-        pltpu.make_async_remote_copy(
-            src_ref=dst,
-            dst_ref=dst,
-            send_sem=send_sem,
-            recv_sem=recv_sem,
-            device_id=device,
-            device_id_type=MESH,
-        ).wait_recv()
-
-    def seq_peer(k):
-        return {"seq": lax.rem(s + k, n_seq)}
-
-    for k in range(1, n_seq):
-        send(xg.at[0], xg.at[k], x_send.at[k], x_recv.at[k], seq_peer(n_seq - k))
-
     for load in loads[3:6]:
         load.wait()
     both = jnp.concatenate([xg[0, i] for i in range(images)], axis=1)
@@ -301,6 +269,38 @@
         + [jnp.zeros((8 - images, toks), F32)],
         axis=0,
     )
+    pl.semaphore_wait(barrier, len(others))
+
+    sends = []
+
+    def send(src, dst, send_sem, recv_sem, device):
+        copy = pltpu.make_async_remote_copy(
+            src_ref=src,
+            dst_ref=dst,
+            send_sem=send_sem,
+            recv_sem=recv_sem,
+            device_id=device,
+            device_id_type=MESH,
+        )
+        copy.start()
+        sends.append(copy)
+
+    def arrive(dst, send_sem, recv_sem, device):
+        pltpu.make_async_remote_copy(
+            src_ref=dst,
+            dst_ref=dst,
+            send_sem=send_sem,
+            recv_sem=recv_sem,
+            device_id=device,
+            device_id_type=MESH,
+        ).wait_recv()
+
+    def seq_peer(k):
+        return {"seq": lax.rem(s + k, n_seq)}
+
+    for k in range(1, n_seq):
+        send(xg.at[0], xg.at[k], x_send.at[k], x_recv.at[k], seq_peer(n_seq - k))
+
     for k in range(1, n_seq):
         send(rg.at[0], rg.at[k], r_send.at[k], r_recv.at[k], seq_peer(n_seq - k))
 

time: 41.9 us -> 41.9 us (level)
  no operation moved by 1% of the time
where the time goes in v5:
time: 41.9 us; the launch traced here: 41.8 us
  Pallas kernels  39 us (93%)
  local copies, waits for them, and re-layouts  2.19 us (5%)
  between operations  0.64 us (2%)
    pallas_call x1, Pallas kernels, per_device(): pl.pallas_call(functools.partial(kernel, (n_group, n_seq, n_dp)), out_sha...  39 us
    unnamed x3, local copies, waits for them, and re-layouts  2.19 us

profile of v5, /device:TPU:1, one launch (start us, length us, event | category | flops | bytes accessed | tf_op | source)
XLA Modules:
  0.0 41.8 jit_solution(1844789384067544570)
XLA Ops:
  0.6 39.0 %shard_map.130 = (f32[2,64,256]{2,1,0:T(8,128)S(1)}, f32[2,64,256]{2,1,0:T(8,128)S(1)}, f32[64,3072]{1,0:T(8,128)S(1)}) custom-call(s32[2]{0:T(128)} %t_hbm.1, bf16[2,64,256]{2,1,0:T(8,128)(2,1)} %bitcast.25, bf16[2,64,256]{2,1,0:T(8,128)(2,1)} %bitcast.26, f32[2,64,256]{2,1,0:T(8,128)} %bitcast.24, bf16[64,3072]{1,0:T(8,128)(2,1)} %bitcast.22, ...), custom_call_target="tpu_custom_call" | custom-call | tf_op jit(solution)/shard_map/pallas_call | solution.py:554
  39.6 0.7 %copy.17 = f32[1,2,256,64]{2,3,1,0:T(8,128)} copy(f32[1,2,256,64]{2,3,1,0:T(8,128)S(1)} %bitcast.20) | data formatting | bytes 262144
  40.3 0.7 %copy.18 = f32[2,256,64]{1,2,0:T(8,128)} copy(f32[2,256,64]{1,2,0:T(8,128)S(1)} %bitcast.19) | data formatting | bytes 262144
  40.9 0.9 %copy.19 = f32[3072,64]{0,1:T(8,128)} copy(f32[3072,64]{0,1:T(8,128)S(1)} %bitcast.18) | data formatting | bytes 1572864
